TPU v7x, 512 devices: a whole 4x4x16 slice. The times are simulated.
512 devices in a mesh: replica: 64 (over y, z_hi, x, core), dp: 8 (over z_lo).
Axes of the slice: x: 4, y: 4, z: 16 (z_hi: 2, z_lo: 8; z = z_hi * 8 + z_lo), core: 2. Of those that a mesh axis runs over, the one named last changes fastest.
Arguments:
- local_weight: float32 [2048, 8192], P(('replica', 'dp')), may hold values from -6 to 6
- adam_first: float32 [2048, 8192], P(('replica', 'dp')), may hold values from -6 to 6
- adam_second: float32 [2048, 8192], P(('replica', 'dp')), may hold values from 0.05 to 2
- hidden_acts: bfloat16 [2, 32, 65536], P(None, None, ('replica', 'dp')), may hold values from -6 to 6
- out_grads: bfloat16 [2, 65536, 8192], P(None, ('replica', 'dp')), may hold values from -0.4375 to 0.4375
- global_weight: float32 [32, 8192], P('dp', 'replica'), may hold values from -6 to 6
- outer_momentum: float32 [32, 8192], P('dp', 'replica'), may hold values from -6 to 6
Outputs:
- new_local: float32 [2048, 8192], P(('replica', 'dp'))
- new_first: float32 [2048, 8192], P(('replica', 'dp'))
- new_second: float32 [2048, 8192], P(('replica', 'dp'))
- new_global: float32 [32, 8192], P('dp', 'replica')
- new_momentum: float32 [32, 8192], P('dp', 'replica')
All inputs are finite; a program needn't handle non-finite values.
Results may differ from a plain program's by a relative error of at most 0.0003.
Values sent between devices are 32-bit elements; how exact they have to be, the bound alone decides.
No kernel may reach another device: no remote copies, remote signals or barrier semaphores. Data moves between devices by JAX's collectives and lax.ppermute only.
A program may use at most 64 MiB of HBM per device.

v0:
```python
import jax
import jax.numpy as jnp
from jax import lax
from jax.sharding import PartitionSpec as P

beta_one = 0.9
beta_two = 0.95
inner_rate = 0.02
decay_rate = 0.1
tiny_eps = 1e-08
outer_rate = 0.7
outer_beta = 0.9
mix_share = 0.5


def body(
    local_weight, adam_first, adam_second, hidden_acts, out_grads, global_weight, outer_momentum
):
    row_total = local_weight.shape[0]
    replicas = lax.axis_size("replica")
    offset = lax.axis_index("dp") * row_total
    steps_count = hidden_acts.shape[0]
    weight = local_weight
    first_moment = adam_first
    second_moment = adam_second
    gradients = []
    for inner_step in range(steps_count):
        activations = hidden_acts[inner_step]
        errors = out_grads[inner_step]
        partials = jnp.dot(activations, errors, preferred_element_type=jnp.float32)
        summed = lax.psum(partials, "dp")
        gradients.append(lax.dynamic_slice_in_dim(summed, offset, row_total, 0))
    for gradient in gradients:
        first_moment = beta_one * first_moment + (1.0 - beta_one) * gradient
        second_moment = beta_two * second_moment + (1.0 - beta_two) * gradient * gradient
        update = first_moment / (jnp.sqrt(second_moment) + tiny_eps)
        weight = weight - inner_rate * (update + decay_rate * weight)
    summed_weights = lax.psum_scatter(weight, "replica", scatter_dimension=1, tiled=True)
    average = summed_weights / replicas
    delta = global_weight - average
    new_momentum = outer_beta * outer_momentum + delta
    new_global = global_weight - outer_rate * (delta + outer_beta * new_momentum)
    gathered = lax.all_gather(new_global, "replica", axis=1, tiled=True)
    new_local = mix_share * weight + (1.0 - mix_share) * gathered
    return (new_local, first_moment, second_moment, new_global, new_momentum)


def solution(mesh):
    placed = (
        P(("replica", "dp"), None),
        P(("replica", "dp"), None),
        P(("replica", "dp"), None),
        P(None, None, ("replica", "dp")),
        P(None, ("replica", "dp"), None),
        P("dp", "replica"),
        P("dp", "replica"),
    )
    return jax.shard_map(
        body,
        mesh=mesh,
        in_specs=placed,
        out_specs=(
            P(("replica", "dp"), None),
            P(("replica", "dp"), None),
            P(("replica", "dp"), None),
            P("dp", "replica"),
            P("dp", "replica"),
        ),
        check_vma=False,
    )
```

profile of v0, /device:TPU:1, one launch (start us, length us, event | category | flops | bytes accessed | tf_op | source)
XLA Modules:
  0.0 895.0 jit_solution(9789959603347147784)
XLA Ops:
  7.2 0.0 copy-start.2
  7.2 0.0 copy-start.1
  7.2 0.0 copy-start
  7.2 0.0 all-reduce.3.cloned.1.call-start
  7.2 3.1 fusion
  10.4 3.0 fusion.2
  13.4 0.0 all-reduce.3.cloned.1.call-update
  13.4 0.0 reduce-scatter.4.cloned.1.call-start
  13.4 141.2 %all-reduce.3.cloned.1.call-done = (f32[32,8192]{1,0:T(8,128)}, f32[32,8192]{1,0:T(8,128)}) async-done(((f32[32,8192]{1,0:T(8,128)}, f32[32,8192]{1,0:T(8,128)}), (f32[32,8192]{1,0:T(8,128)}, f32[32,8192]{1,0:T(8,128)})) %all-reduce.3.cloned.1.call-update) | async-done | bytes 2097168 | tf_op jit(solution)/shard_map/psum | solution.py:31
  154.6 0.0 copy-done.2
  154.6 0.0 copy-done.1
  154.6 0.0 copy-done
  154.6 2.1 multiply_subtract_fusion
  156.8 0.0 copy-start.4
  156.8 0.0 copy-start.5
  156.8 2.6 copy.12
  159.4 0.0 reduce-scatter.4.cloned.1.call-update
  159.4 565.7 %reduce-scatter.4.cloned.1.call-done = f32[128,4]{1,0:T(8,128)} async-done(((f32[8192,4]{1,0:T(8,128)}), f32[128,4]{1,0:T(8,128)}) %reduce-scatter.4.cloned.1.call-update) | async-done | bytes 2064
  725.2 0.9 copy.13
  726.1 0.0 copy-done.4
  726.1 0.0 copy-done.5
  726.1 0.6 multiply_subtract_fusion.1
  726.7 0.0 copy-start.3
  726.7 160.8 %all_gather.3 = f32[4,8192]{1,0:T(4,128)S(1)} all-gather(f32[4,128]{1,0:T(4,128)S(1)} %get-tuple-element.7), channel_id=1, replica_groups=mesh['replica'=64,'dp'=8] {'replica'}, dimensions={1}, use_global_device_ids=true | all-gather | bytes 133120 | tf_op jit(solution)/shard_map/all_gather | solution.py:43
  887.5 0.7 add_multiply_fusion
  888.2 0.0 copy-done.3
Async XLA Ops:
  7.2 147.5 %copy-start.2 = (f32[4,8192]{1,0:T(4,128)S(1)}, f32[4,8192]{1,0:T(4,128)}, u32[]{:S(2)}) copy-start(f32[4,8192]{1,0:T(4,128)} %param.9) | copy-start | bytes 393220
  7.2 147.5 %copy-start.1 = (f32[4,8192]{1,0:T(4,128)S(1)}, f32[4,8192]{1,0:T(4,128)}, u32[]{:S(2)}) copy-start(f32[4,8192]{1,0:T(4,128)} %param.8) | copy-start | bytes 393220
  7.2 147.5 %copy-start = (f32[4,8192]{1,0:T(4,128)S(1)}, f32[4,8192]{1,0:T(4,128)}, u32[]{:S(2)}) copy-start(f32[4,8192]{1,0:T(4,128)} %param.7) | copy-start | bytes 393220
  7.2 147.4 %all-reduce.3.cloned.1.call-start = ((), (), s32[]{:S(2)}) async-start(), calls=%async_computation.2 | async-start | bytes 4194304 | tf_op jit(solution)/shard_map/psum | solution.py:31
  13.4 711.8 %reduce-scatter.4.cloned.1.call-start = ((), (), s32[]{:S(2)}) async-start(), calls=%async_computation.1 | async-start | bytes 4259840
  156.8 569.3 %copy-start.4 = (f32[4,128]{1,0:T(4,128)S(1)}, f32[4,128]{1,0:T(4,128)}, u32[]{:S(2)}) copy-start(f32[4,128]{1,0:T(4,128)} %param.12) | copy-start | bytes 6148
  156.8 569.3 %copy-start.5 = (f32[4,128]{1,0:T(4,128)S(1)}, f32[4,128]{1,0:T(4,128)}, u32[]{:S(2)}) copy-start(f32[4,128]{1,0:T(4,128)} %param.13) | copy-start | bytes 6148
  726.7 161.5 %copy-start.3 = (f32[4,128]{1,0:T(4,128)}, f32[4,128]{1,0:T(4,128)S(1)}, u32[]{:S(2)}) copy-start(f32[4,128]{1,0:T(4,128)S(1)} %get-tuple-element.7) | copy-start | bytes 6148
Sparse Core Ops, SparseCore 0:
  13.5 141.0 all-reduce.2
  159.5 565.5 reduce-scatter.3
where the time goes:
time: 895 us
  waiting for transfers between devices  707 us (79%)
  blocking collectives  161 us (18%)
  between operations  14.1 us (2%)
    unnamed x3, waiting for transfers between devices  566 us
    all_gather x1, blocking collectives, body(): gathered = lax.all_gather(new_global, 'replica', axis=1, tiled=True)  161 us
    psum x1, waiting for transfers between devices, body(): summed = lax.psum(partials, 'dp')  141 us
  transfers between devices with their start and end apart: 2, of which 2 were waited for; matrix products, arithmetic and copies ran while one was open for 0% of the time, Pallas kernels for 0%

commit v1 on v0

--- a/solution.py
+++ b/solution.py
@@ -28,7 +28,7 @@
         activations = hidden_acts[inner_step]
         errors = out_grads[inner_step]
         partials = jnp.dot(activations, errors, preferred_element_type=jnp.float32)
-        summed = lax.psum(partials, "dp")
+        summed = jnp.sum(lax.all_gather(partials, "dp"), axis=0)
         gradients.append(lax.dynamic_slice_in_dim(summed, offset, row_total, 0))
     for gradient in gradients:
         first_moment = beta_one * first_moment + (1.0 - beta_one) * gradient

time: 895 us -> 1120 us (1.25)
  waiting for transfers between devices: 707 us -> 921 us
    all_gather x0 -> x2, waiting for transfers between devices: none -> 360 us  [body(): summed = jnp.sum(lax.all_gather(partials, 'dp'), axis=0)]
    psum x1 -> x0, waiting for transfers between devices: 141 us -> none  [body(): summed = lax.psum(partials, 'dp')]
    unnamed x3 -> x4, waiting for transfers between devices: 566 us -> 561 us
  transfers between devices with their start and end apart: 2 -> 3, of which waited for: 2 -> 3; matrix products, arithmetic and copies ran while one was open for 0% -> 1% of each run, Pallas kernels for 0% -> 0%
where the time goes in v1:
time: 1120 us
  waiting for transfers between devices  921 us (82%)
  blocking collectives  161 us (14%)
  between operations  13.8 us (1%)
    unnamed x4, waiting for transfers between devices  561 us
    all_gather x2, waiting for transfers between devices, body(): summed = jnp.sum(lax.all_gather(partials, 'dp'), axis=0)  360 us
    all_gather x1, blocking collectives, body(): gathered = lax.all_gather(new_global, 'replica', axis=1, tiled=True)  161 us
  transfers between devices with their start and end apart: 3, of which 3 were waited for; matrix products, arithmetic and copies ran while one was open for 1% of the time, Pallas kernels for 0%

profile of v1, /device:TPU:1, one launch (start us, length us, event | category | flops | bytes accessed | tf_op | source)
XLA Modules:
  0.0 1116.1 jit_solution(7245292388235839359)
XLA Ops:
  7.2 0.0 copy-start.3
  7.2 0.0 all-gather.7.cloned.1.call-start
  7.2 3.0 fusion
  10.3 0.0 all-gather.7.cloned.1.call-update
  10.3 0.0 all-gather.5.cloned.1.call-start
  10.3 0.0 copy-done.3
  10.3 3.0 fusion.2
  13.3 0.0 all-gather.5.cloned.1.call-update
  13.3 0.0 reduce-scatter.4.cloned.1.call-start
  13.4 184.0 %all-gather.7.cloned.1.call-done = f32[256,8192]{1,0:T(8,128)} async-done(((f32[32,8192]{1,0:T(8,128)}), f32[256,8192]{1,0:T(8,128)}) %all-gather.7.cloned.1.call-update) | async-done | bytes 8388624 | tf_op jit(solution)/shard_map/all_gather | solution.py:31
  197.4 3.9 reduce_sum.19
  201.3 175.9 %all-gather.5.cloned.1.call-done = f32[256,8192]{1,0:T(8,128)} async-done(((f32[32,8192]{1,0:T(8,128)}), f32[256,8192]{1,0:T(8,128)}) %all-gather.5.cloned.1.call-update) | async-done | bytes 8388624 | tf_op jit(solution)/shard_map/all_gather | solution.py:31
  377.2 0.0 copy-start
  377.2 0.0 copy-start.1
  377.2 0.0 copy-start.2
  377.2 4.0 reduce_sum.18
  381.2 0.0 copy-done
  381.2 0.0 copy-done.1
  381.2 0.0 copy-done.2
  381.2 1.1 multiply_subtract_fusion
  382.3 0.0 copy-start.5
  382.3 0.0 copy-start.6
  382.3 2.6 copy.12
  385.0 0.0 reduce-scatter.4.cloned.1.call-update
  385.0 561.0 %reduce-scatter.4.cloned.1.call-done = f32[128,4]{1,0:T(8,128)} async-done(((f32[8192,4]{1,0:T(8,128)}), f32[128,4]{1,0:T(8,128)}) %reduce-scatter.4.cloned.1.call-update) | async-done | bytes 2064
  946.0 0.9 copy.13
  946.9 0.0 copy-done.5
  946.9 0.0 copy-done.6
  946.9 0.6 multiply_subtract_fusion.1
  947.5 0.0 copy-start.4
  947.5 161.3 %all_gather.19 = f32[4,8192]{1,0:T(4,128)S(1)} all-gather(f32[4,128]{1,0:T(4,128)S(1)} %get-tuple-element.5), channel_id=1, replica_groups=mesh['replica'=64,'dp'=8] {'replica'}, dimensions={1}, use_global_device_ids=true | all-gather | bytes 133120 | tf_op jit(solution)/shard_map/all_gather | solution.py:43
  1108.8 0.7 add_multiply_fusion
  1109.5 0.0 copy-done.4
Async XLA Ops:
  7.2 3.2 copy-start.3
  7.2 190.3 %all-gather.7.cloned.1.call-start = ((), (), s32[]{:S(2)}) async-start(), calls=%async_computation.2 | async-start | bytes 9437184 | tf_op jit(solution)/shard_map/all_gather | solution.py:31
  10.3 366.9 %all-gather.5.cloned.1.call-start = ((), (), s32[]{:S(2)}) async-start(), calls=%async_computation.1 | async-start | bytes 9437184 | tf_op jit(solution)/shard_map/all_gather | solution.py:31
  13.3 932.7 %reduce-scatter.4.cloned.1.call-start = ((), (), s32[]{:S(2)}) async-start(), calls=%async_computation.3 | async-start | bytes 4259840
  377.2 4.0 copy-start
  377.2 4.0 copy-start.1
  377.2 4.0 copy-start.2
  382.3 564.6 %copy-start.5 = (f32[4,128]{1,0:T(4,128)S(1)}, f32[4,128]{1,0:T(4,128)}, u32[]{:S(2)}) copy-start(f32[4,128]{1,0:T(4,128)} %param.12) | copy-start | bytes 6148
  382.3 564.6 %copy-start.6 = (f32[4,128]{1,0:T(4,128)S(1)}, f32[4,128]{1,0:T(4,128)}, u32[]{:S(2)}) copy-start(f32[4,128]{1,0:T(4,128)} %param.13) | copy-start | bytes 6148
  947.5 162.0 %copy-start.4 = (f32[4,128]{1,0:T(4,128)}, f32[4,128]{1,0:T(4,128)S(1)}, u32[]{:S(2)}) copy-start(f32[4,128]{1,0:T(4,128)S(1)} %get-tuple-element.5) | copy-start | bytes 6148
Sparse Core Ops, SparseCore 0:
  10.4 186.9 all-gather.6
  199.5 177.6 all-gather.4
  385.1 560.8 reduce-scatter.3

commit v2 on v0

--- a/solution.py
+++ b/solution.py
@@ -40,7 +40,9 @@
     delta = global_weight - average
     new_momentum = outer_beta * outer_momentum + delta
     new_global = global_weight - outer_rate * (delta + outer_beta * new_momentum)
-    gathered = lax.all_gather(new_global, "replica", axis=1, tiled=True)
+    gathered = jnp.concatenate(
+        lax.all_to_all(jnp.stack([new_global] * lax.axis_size("replica")), "replica", 0, 0), axis=1
+    )
     new_local = mix_share * weight + (1.0 - mix_share) * gathered
     return (new_local, first_moment, second_moment, new_global, new_momentum)
 

time: 895 us -> 771 us (0.86)
  blocking collectives: 161 us -> 35.6 us
    all_gather x1 -> x0, blocking collectives: 161 us -> none  [body(): gathered = lax.all_gather(new_global, 'replica', axis=1, tiled=True)]
    all_to_all x0 -> x1, blocking collectives: none -> 35.6 us  [body(): lax.all_to_all(jnp.stack([new_global] * lax.axis_size('replica')), 'repli...]
where the time goes in v2:
time: 771 us; the launch traced here: 770 us
  waiting for transfers between devices  707 us (92%)
  blocking collectives  35.6 us (5%)
  between operations  14.1 us (2%)
    unnamed x3, waiting for transfers between devices  566 us
    psum x1, waiting for transfers between devices, body(): summed = lax.psum(partials, 'dp')  141 us
    all_to_all x1, blocking collectives, body(): lax.all_to_all(jnp.stack([new_global] * lax.axis_size('replica')), 'repli...  35.6 us
  transfers between devices with their start and end apart: 2, of which 2 were waited for; matrix products, arithmetic and copies ran while one was open for 0% of the time, Pallas kernels for 0%

profile of v2, /device:TPU:1, one launch (start us, length us, event | category | flops | bytes accessed | tf_op | source)
XLA Modules:
  0.0 769.8 jit_solution(8961845156219731723)
XLA Ops:
  7.2 0.0 copy-start.2
  7.2 0.0 copy-start.1
  7.2 0.0 copy-start
  7.2 0.0 all-reduce.3.cloned.1.call-start
  7.2 3.1 fusion
  10.4 3.0 fusion.2
  13.4 0.0 all-reduce.3.cloned.1.call-update
  13.4 0.0 reduce-scatter.4.cloned.1.call-start
  13.4 141.2 %all-reduce.3.cloned.1.call-done = (f32[32,8192]{1,0:T(8,128)}, f32[32,8192]{1,0:T(8,128)}) async-done(((f32[32,8192]{1,0:T(8,128)}, f32[32,8192]{1,0:T(8,128)}), (f32[32,8192]{1,0:T(8,128)}, f32[32,8192]{1,0:T(8,128)})) %all-reduce.3.cloned.1.call-update) | async-done | bytes 2097168 | tf_op jit(solution)/shard_map/psum | solution.py:31
  154.6 0.0 copy-done.2
  154.6 0.0 copy-done.1
  154.6 0.0 copy-done
  154.6 2.1 multiply_subtract_fusion
  156.8 0.0 copy-start.4
  156.8 0.0 copy-start.5
  156.8 2.6 copy.12
  159.4 0.0 reduce-scatter.4.cloned.1.call-update
  159.4 565.7 %reduce-scatter.4.cloned.1.call-done = f32[128,4]{1,0:T(8,128)} async-done(((f32[8192,4]{1,0:T(8,128)}), f32[128,4]{1,0:T(8,128)}) %reduce-scatter.4.cloned.1.call-update) | async-done | bytes 2064
  725.1 0.9 copy.13
  726.0 0.0 copy-done.4
  726.0 0.0 copy-done.5
  726.0 0.6 multiply_subtract_fusion.1
  726.6 0.0 copy-start.3
  726.7 35.6 %all_to_all.5 = f32[64,4,128]{2,1,0:T(4,128)S(1)} all-to-all(f32[64,4,128]{2,1,0:T(4,128)S(1)} %stack.2), channel_id=1, replica_groups=mesh['replica'=64,'dp'=8] {'replica'}, dimensions={0} | all-to-all | bytes 262144 | tf_op jit(solution)/shard_map/all_to_all | solution.py:44
  762.2 0.7 fusion.8
  762.9 0.0 copy-done.3
  (1 shorter events, 0.0 us)
Async XLA Ops:
  7.2 147.5 %copy-start.2 = (f32[4,8192]{1,0:T(4,128)S(1)}, f32[4,8192]{1,0:T(4,128)}, u32[]{:S(2)}) copy-start(f32[4,8192]{1,0:T(4,128)} %param.9) | copy-start | bytes 393220
  7.2 147.5 %copy-start.1 = (f32[4,8192]{1,0:T(4,128)S(1)}, f32[4,8192]{1,0:T(4,128)}, u32[]{:S(2)}) copy-start(f32[4,8192]{1,0:T(4,128)} %param.8) | copy-start | bytes 393220
  7.2 147.5 %copy-start = (f32[4,8192]{1,0:T(4,128)S(1)}, f32[4,8192]{1,0:T(4,128)}, u32[]{:S(2)}) copy-start(f32[4,8192]{1,0:T(4,128)} %param.7) | copy-start | bytes 393220
  7.2 147.4 %all-reduce.3.cloned.1.call-start = ((), (), s32[]{:S(2)}) async-start(), calls=%async_computation.3 | async-start | bytes 4194304 | tf_op jit(solution)/shard_map/psum | solution.py:31
  13.4 711.7 %reduce-scatter.4.cloned.1.call-start = ((), (), s32[]{:S(2)}) async-start(), calls=%async_computation.2 | async-start | bytes 4259840
  156.8 569.3 %copy-start.4 = (f32[4,128]{1,0:T(4,128)S(1)}, f32[4,128]{1,0:T(4,128)}, u32[]{:S(2)}) copy-start(f32[4,128]{1,0:T(4,128)} %param.12) | copy-start | bytes 6148
  156.8 569.3 %copy-start.5 = (f32[4,128]{1,0:T(4,128)S(1)}, f32[4,128]{1,0:T(4,128)}, u32[]{:S(2)}) copy-start(f32[4,128]{1,0:T(4,128)} %param.13) | copy-start | bytes 6148
  726.6 36.3 %copy-start.3 = (f32[4,128]{1,0:T(4,128)}, f32[4,128]{1,0:T(4,128)S(1)}, u32[]{:S(2)}) copy-start(f32[4,128]{1,0:T(4,128)S(1)} %get-tuple-element.7) | copy-start | bytes 6148
Sparse Core Ops, SparseCore 0:
  13.5 141.0 all-reduce.2
  159.5 565.5 reduce-scatter.3
